TPU v7x, 512 devices: a whole 4x8x8 slice. The times are simulated.
512 devices in a mesh: prow: 64 (over z_lo, x, y), pcol: 8 (over z_hi, core).
Axes of the slice: x: 4, y: 8, z: 8 (z_hi: 4, z_lo: 2; z = z_hi * 2 + z_lo), core: 2. Of those that a mesh axis runs over, the one named last changes fastest.
Arguments:
- ancestor_inverse: float32 [3840, 3840], P('pcol', 'prow'), as said below
- factor: float32 [3840, 16384], P('pcol', 'prow'), may hold values from -0.75 to 0.75
- struct_rows: int32 [64, 11], P('prow'), may hold values from 0 to 14, all different within a row
- diag_factor_inverse: float32 [64, 256, 256], P('prow', 'pcol'), may hold values from -0.375 to 0.375
Outputs:
- selected_inverse: float32 [3840, 16384], P('pcol', 'prow')
- diag_inverse: float32 [64, 256, 256], P('prow', 'pcol')
Inputs may be any that keep to these rules, and one draw needn't show every extreme that they name: `struct_rows`: each row lists 11 different ancestor blocks, and every ancestor block is listed by some supernode. ancestor_inverse is symmetric.
All inputs are finite; a program needn't handle non-finite values.
Results may differ from a plain program's by a relative error of at most 0.000073.
Values sent between devices are 32-bit elements; how exact they have to be, the bound alone decides.
A program may use at most 64 MiB of HBM per device.

v0:
```python
import jax
import jax.numpy as jnp
from jax import lax
from jax.sharding import PartitionSpec as P

HIGHEST = lax.Precision.HIGHEST


def on_device(ancestor_inverse, factor, struct_rows, diag_factor_inverse):
    slab_rows = factor.shape[0]
    block_width = diag_factor_inverse.shape[2]
    local_supers = struct_rows.shape[0]
    column_index = lax.axis_index("pcol")
    row_ids = column_index * slab_rows + jnp.arange(slab_rows, dtype=jnp.int32)
    block_ids = row_ids // block_width
    present = jnp.any(block_ids[:, None, None] == struct_rows[None, :, :], axis=2).astype(
        jnp.float32
    )
    factor_used = (
        factor.reshape(slab_rows, local_supers, block_width) * present[:, :, None]
    ).reshape(slab_rows, local_supers * block_width)
    full_panel = lax.all_gather(factor_used, "pcol", axis=0, tiled=True)
    product = jnp.dot(
        lax.all_gather(ancestor_inverse, "prow", axis=1, tiled=True),
        full_panel,
        precision=HIGHEST,
        preferred_element_type=jnp.float32,
    )
    selected = -(product.reshape(slab_rows, local_supers, block_width) * present[:, :, None])
    inner_part = jnp.einsum(
        "rkc,rkd->kcd",
        factor_used.reshape(slab_rows, local_supers, block_width),
        selected,
        precision=HIGHEST,
        preferred_element_type=jnp.float32,
    )
    diag_rows = diag_factor_inverse.shape[1]
    row_pos = column_index * diag_rows + jnp.arange(diag_rows, dtype=jnp.int32)
    lower_mask = row_pos[:, None] >= jnp.arange(block_width, dtype=jnp.int32)[None, :]
    lower_part = jnp.where(lower_mask[None, :, :], diag_factor_inverse, 0.0)
    gram_part = jnp.einsum(
        "kmc,kmd->kcd",
        lower_part,
        lower_part,
        precision=HIGHEST,
        preferred_element_type=jnp.float32,
    )
    diag_block = lax.psum_scatter(gram_part - inner_part, "pcol", scatter_dimension=1, tiled=True)
    return (selected.reshape(slab_rows, local_supers * block_width), diag_block)


def solution(mesh):
    placed = (P("pcol", "prow"), P("pcol", "prow"), P("prow", None), P("prow", "pcol", None))
    return jax.shard_map(
        on_device,
        mesh=mesh,
        in_specs=placed,
        out_specs=(P("pcol", "prow"), P("prow", "pcol", None)),
        check_vma=False,
    )
```

profile of v0, /device:TPU:1, one launch (start us, length us, event | category | flops | bytes accessed | tf_op | source)
XLA Modules:
  0.0 445.3 jit_solution(15549665785883387425)
XLA Ops:
  7.2 0.0 all-gather.6.cloned.1.call-start
  7.2 0.7 all-gather.6.cloned.1.call-update
  7.9 0.0 all-gather.4.cloned.1.call-start
  8.0 0.7 compare_reduce_fusion
  8.7 1.9 broadcast_multiply_fusion
  10.7 0.0 all-gather.4.cloned.1.call-update
  10.7 0.0 reduce-scatter.2.cloned.1.call-start
  10.8 1.3 fusion.2
  12.1 281.2 %all-gather.6.cloned.1.call-done = f32[64,60,480]{2,1,0:T(8,128)} async-done(((f32[1,60,480]{2,1,0:T(8,128)}), f32[64,60,480]{2,1,0:T(8,128)}) %all-gather.6.cloned.1.call-update) | async-done | bytes 7372816 | tf_op jit(solution)/shard_map/all_gather | solution.py:24
  293.2 8.6 %reshape.139 = f32[3840,480]{1,0:T(8,128)} reshape(f32[64,60,480]{2,1,0:T(8,128)} %all-gather.6.cloned.1.call-done) | data formatting | bytes 14745600
  301.8 0.0 copy-start
  301.8 83.0 %all-gather.4.cloned.1.call-done = f32[3840,256]{1,0:T(8,128)} async-done(((f32[480,256]{1,0:T(8,128)}), f32[3840,256]{1,0:T(8,128)}) %all-gather.4.cloned.1.call-update) | async-done | bytes 3932176 | tf_op jit(solution)/shard_map/all_gather | solution.py:22
  384.8 16.1 %fusion = f32[256,480]{0,1:T(8,128)S(1)} fusion(f32[3840,256]{1,0:T(8,128)} %all-gather.4.cloned.1.call-done, f32[3840,480]{1,0:T(8,128)} %reshape.139, f32[480]{0:T(512)S(1)} %convert_element_type.9), kind=kOutput, calls=%fused_computation.1 | convolution fusion | flops 5662556160 | bytes 11798400 | tf_op jit(solution)/shard_map/dot_general | solution.py:23
  400.9 0.0 copy-done
  400.9 0.0 copy-start.1
  400.9 1.7 fusion.1
  402.6 0.0 reduce-scatter.2.cloned.1.call-update
  402.7 36.0 %reduce-scatter.2.cloned.1.call-done = f32[1,32,256]{2,1,0:T(8,128)} async-done(((f32[1,256,256]{2,1,0:T(8,128)}), f32[1,32,256]{2,1,0:T(8,128)}) %reduce-scatter.2.cloned.1.call-update) | async-done | bytes 32784 | tf_op jit(solution)/shard_map/reduce_scatter | solution.py:48
  438.7 0.0 copy-done.1
  (3 shorter events, 0.0 us)
Async XLA Ops:
  7.2 286.1 %all-gather.6.cloned.1.call-start = ((), (), s32[]{:S(2)}) async-start(), calls=%async_computation.3 | async-start | bytes 8519680 | tf_op jit(solution)/shard_map/all_gather | solution.py:24
  7.9 376.9 %all-gather.4.cloned.1.call-start = ((), (), s32[]{:S(2)}) async-start(), calls=%async_computation.1 | async-start | bytes 4423680 | tf_op jit(solution)/shard_map/all_gather | solution.py:22
  10.7 428.0 %reduce-scatter.2.cloned.1.call-start = ((), (), s32[]{:S(2)}) async-start(), calls=%async_computation.2 | async-start | bytes 294912 | tf_op jit(solution)/shard_map/reduce_scatter | solution.py:48
  301.8 99.1 %copy-start = (f32[480,256]{1,0:T(8,128)S(1)}, f32[480,256]{1,0:T(8,128)}, u32[]{:S(2)}) copy-start(f32[480,256]{1,0:T(8,128)} %broadcast_multiply_fusion) | copy-start | bytes 1474564
  400.9 37.8 %copy-start.1 = (f32[256,480]{0,1:T(8,128)}, f32[256,480]{0,1:T(8,128)S(1)}, u32[]{:S(2)}) copy-start(f32[256,480]{0,1:T(8,128)S(1)} %fusion) | copy-start | bytes 1474564
Sparse Core Ops, SparseCore 0:
  10.1 283.1 all-gather.5
  295.9 88.8 all-gather.3
  402.8 35.8 reduce-scatter.1
where the time goes:
time: 447 us; the launch traced here: 445 us
  waiting for transfers between devices  401 us (90%)
  matrix products  19.1 us (4%)
  between operations  13.8 us (3%)
  local copies, waits for them, and re-layouts  8.59 us (2%)
    all_gather x1, waiting for transfers between devices, on_device(): lax.all_gather(ancestor_inverse, 'prow', axis=1, tiled=True)  281 us
    all_gather x1, waiting for transfers between devices, on_device(): full_panel = lax.all_gather(factor_used, 'pcol', axis=0, tiled=True)  83 us
    reduce_scatter x1, waiting for transfers between devices, on_device(): lax.psum_scatter(gram_part - inner_part, 'pcol', scatter_dimension=1, til...  36 us
    dot_general x1, matrix products, on_device(): jnp.dot(lax.all_gather(ancestor_inverse, 'prow', axis=1, tiled=True), ful...  16.1 us
  transfers between devices with their start and end apart: 3, of which 3 were waited for; matrix products, arithmetic and copies ran while one was open for 3% of the time, Pallas kernels for 0%

commit v1 on v0

v1 whole, which is shorter than its diff:
```python
import jax
import jax.numpy as jnp
import numpy as np
from jax import lax
from jax.experimental import pallas as pl
from jax.experimental.pallas import tpu as pltpu
from jax.sharding import PartitionSpec as P

MESH = pl.DeviceIdType.MESH
F32 = jnp.float32
BF16 = jnp.bfloat16
NX, NY, NZ = 4, 8, 8
B = 256
SLAB = 480
HALF = 240
U0 = 96
U1 = 144


def split(v):
    high = v.astype(BF16)
    return high, (v - high.astype(F32)).astype(BF16)


def dot3(left, right, dims):
    lh, ll = left
    rh, rl = right
    go = lambda p, q: lax.dot_general(p, q, (dims, ((), ())), preferred_element_type=F32)
    return go(lh, rh) + (go(ll, rh) + go(lh, rl))


def kernel(
    a_ref, f_ref, s_ref, d_ref, sel_ref, diag_ref,
    tz, pk, st, ag0, ag1, ah, al, fu, fg, fph, fpl, acc, cr, lb, part, dr,
    send, r_a0, r_x0, r_y1, r_y0, r_x1, r_s0, r_s1, r_f, r_l, r_c, r_d,
):
    def rem(value, by):
        return lax.rem(value, np.int32(by))

    def div(value, by):
        return lax.div(value, np.int32(by))

    r, p = lax.axis_index("prow"), lax.axis_index("pcol")
    a, x, y = div(r, 32), rem(div(r, 8), 4), rem(r, 8)
    zh, c = div(p, 2), rem(p, 2)
    z = 2 * zh + a
    eq, ne = a == c, a != c
    dsg = 1 - 2 * c
    xp, xm, x2 = rem(x + 4 + dsg, 4), rem(x + 4 - dsg, 4), rem(x + 2, 4)

    def yy(k):
        return rem(y + 16 + k * dsg, 8)

    def zz(k):
        return rem(z + 8 + k, 8)

    def dev(x_, y_, z_, c_):
        return (rem(z_, 2) * 32 + x_ * 8 + y_, div(z_, 2) * 2 + c_)

    counter = [0]
    pending = {"all": [], "eq": [], "ne": []}

    def go(src, dst, recv, device, kind="all"):
        copy = pltpu.make_async_remote_copy(
            src_ref=src, dst_ref=dst, send_sem=send.at[counter[0]], recv_sem=recv,
            device_id=device, device_id_type=MESH,
        )
        counter[0] += 1
        copy.start()
        pending[kind].append((src.shape, counter[0] - 1))

    sibling = dev(x, y, z, 1 - c)

    def arrived(dst, recv):
        pltpu.make_async_remote_copy(
            src_ref=dst, dst_ref=dst, send_sem=send.at[0], recv_sem=recv,
            device_id=sibling, device_id_type=MESH,
        ).wait_recv()

    barrier = pltpu.get_barrier_semaphore()
    greeted = [sibling]
    for k in range(1, NZ):
        greeted += [dev(x, y, zz(k), 0), dev(x, y, zz(k), 1)]
    greeted += [dev(xp, y, z, c), dev(xm, y, z, c), dev(x, yy(1), z, c), dev(x, yy(-1), z, c)]
    for device in greeted:
        pl.semaphore_signal(barrier, inc=1, device_id=device, device_id_type=MESH)

    tz[...] = jnp.zeros_like(tz)
    tz[:, 0:60] = a_ref[...]
    for h in range(2):
        pk[h] = tz[HALF * h : HALF * h + 120, :] + pltpu.roll(tz[HALF * h + 120 : HALF * h + 240, :], 64, 1)

    first = div(SLAB * p, B)

    def listed(block):
        total = np.float32(0.0)
        for i in range(s_ref.shape[1]):
            total = jnp.maximum(total, jnp.where(s_ref[0, i] == block, np.float32(1.0), np.float32(0.0)))
        return total

    present = [listed(first + i) for i in range(3)]

    def masked(value):
        block = (lax.broadcasted_iota(jnp.int32, (SLAB, B), 0) + SLAB * p) // B - first
        return value * jnp.where(block == 0, present[0], jnp.where(block == 1, present[1], present[2]))

    fu[...] = masked(f_ref[...])

    @pl.when(eq)
    def _():
        fg[p, 0:SLAB, :] = fu[...]
        st[a] = pk[c]

    for j in range(8):
        fg[j, SLAB : SLAB + 8, :] = jnp.zeros((8, B), F32)
    row = lax.broadcasted_iota(jnp.int32, (32, B), 0) + 32 * p
    lb[0] = jnp.where(row >= lax.broadcasted_iota(jnp.int32, (32, B), 1), d_ref[0], 0.0)
    acc[...] = jnp.zeros_like(acc)

    pl.semaphore_wait(barrier, len(greeted))

    @pl.when(eq)
    def _():
        go(pk.at[1 - c], st.at[a], r_a0.at[a], sibling, "eq")

    @pl.when(ne)
    def _():
        for h in range(2):
            go(pk.at[h], st.at[a], r_a0.at[a], dev(x, y, 2 * zh + c, h), "ne")

    def fslot(j, q):
        return fg.at[j, pl.ds(HALF * q, HALF), :]

    for q in range(2):
        for sign in (1, -1):
            go(fu.at[pl.ds(HALF * q, HALF), :], fslot(p, q), r_f.at[2 * p + q], dev(x, y, zz(sign), a))

    @pl.when(ne)
    def _():
        for q in range(2):
            go(fu.at[pl.ds(HALF * q, HALF), :], fslot(p, q), r_f.at[2 * p + q], sibling, "ne")
        go(lb.at[0], lb.at[1], r_l.at[0], sibling, "ne")

    def f_wait(source, s, q):
        j = 2 * div(source, 2) + s
        arrived(fslot(j, q), r_f.at[2 * j + q])
        return j

    def f_pass(e, distance, sign, kind):
        s, q = e % 2, e // 2
        j = f_wait(zz(-distance * sign), s, q)
        go(fslot(j, q), fslot(j, q), r_f.at[2 * j + q], dev(x, y, zz(sign), c), kind)

    def f1(e):
        @pl.when(ne)
        def _():
            for sign in (1, -1):
                f_pass(e, 1, sign, "ne")

    def f2(e):
        @pl.when(eq)
        def _():
            for sign in (1, -1):
                f_pass(e, 2, sign, "eq")

    def f3(e):
        @pl.when(ne)
        def _():
            s, q = e % 2, e // 2
            way = dsg if e < 3 else -dsg
            j = f_wait(zz(8 - 3 * way), s, q)
            go(fslot(j, q), fslot(j, q), r_f.at[2 * j + q], dev(x, y, zz(way), c), "ne")
            f_wait(zz(3 * way), s, q)

    @pl.when(ne)
    def _():
        arrived(st.at[0], r_a0.at[0])
        arrived(st.at[1], r_a0.at[1])

    @pl.when(eq)
    def _():
        arrived(st.at[1 - a], r_a0.at[1 - a])

    low = lax.broadcasted_iota(jnp.int32, (120, 128), 1) < 64
    p0, p1 = st[0], st[1]
    top = jnp.where(low, p0, pltpu.roll(p1, 64, 1))
    bottom = jnp.where(low, pltpu.roll(p0, 64, 1), p1)
    ag0[c, y, x] = top[0:U0]
    ag1[c, x, y, 0 : 120 - U0, :] = top[U0:120]
    ag1[c, x, y, 120 - U0 : U1, :] = bottom

    yp, ym = yy(1), yy(-1)
    to_xp, to_xm = dev(xp, y, z, c), dev(xm, y, z, c)
    to_yp, to_ym = dev(x, yp, z, c), dev(x, ym, z, c)

    def tile0(x_):
        return ag0.at[c, y, x_]

    def tile1(y_):
        return ag1.at[c, x, y_]

    def bundle0(y_):
        return ag0.at[c, y_]

    def bundle1(x_, half):
        return ag1.at[c, x_, pl.ds(4 * half, 4)]

    def share0(y_):
        go(bundle0(y_), bundle0(y_), r_s0.at[y_], sibling)

    def share1(x_, half):
        go(bundle1(x_, half), bundle1(x_, half), r_s1.at[2 * x_ + half], sibling)

    go(tile0(x), tile0(x), r_x0.at[0], to_xp)
    go(tile0(x), tile0(x), r_x0.at[1], to_xm)
    go(tile1(y), tile1(y), r_y1.at[0], to_yp)
    go(tile1(y), tile1(y), r_y1.at[4], to_ym)

    def y_step(k, part_of, sems, share):
        arrived(part_of(yy(-k)), sems.at[k - 1])
        if k < 4:
            go(part_of(yy(-k)), part_of(yy(-k)), sems.at[k], to_yp)
            arrived(part_of(yy(k)), sems.at[3 + k])
            if k < 3:
                go(part_of(yy(k)), part_of(yy(k)), sems.at[4 + k], to_ym)
        if share is not None:
            share(yy(-k))
            if k < 4:
                share(yy(k))

    arrived(tile0(xm), r_x0.at[0])
    go(tile0(xm), tile0(xm), r_x0.at[2], to_xp)
    y_step(1, tile1, r_y1, None)
    f1(0)
    arrived(tile0(xp), r_x0.at[1])
    arrived(tile0(x2), r_x0.at[2])
    go(bundle0(y), bundle0(y), r_y0.at[0], to_yp)
    go(bundle0(y), bundle0(y), r_y0.at[4], to_ym)
    share0(y)
    y_step(2, tile1, r_y1, None)
    f1(1)
    y_step(3, tile1, r_y1, None)
    f1(2)
    y_step(4, tile1, r_y1, None)
    go(bundle1(x, 0), bundle1(x, 0), r_x1.at[0], to_xp)
    go(bundle1(x, 1), bundle1(x, 1), r_x1.at[2], to_xm)
    go(bundle1(x, 1), bundle1(x, 1), r_x1.at[1], to_xp)
    go(bundle1(x, 0), bundle1(x, 0), r_x1.at[3], to_xm)
    share1(x, 0)
    share1(x, 1)
    y_step(1, bundle0, r_y0, share0)
    f1(3)
    arrived(bundle1(xm, 0), r_x1.at[0])
    go(bundle1(xm, 0), bundle1(xm, 0), r_x1.at[4], to_xp)
    arrived(bundle1(xp, 1), r_x1.at[2])
    go(bundle1(xp, 1), bundle1(xp, 1), r_x1.at[5], to_xm)
    share1(xm, 0)
    share1(xp, 1)
    y_step(2, bundle0, r_y0, share0)

    part[...] = jnp.zeros_like(part)

    @pl.when(eq)
    def _():
        arrived(lb.at[1], r_l.at[0])
        total = jnp.zeros((B, B), F32)
        for i in range(2):
            piece = split(lb[i])
            total = total + dot3(piece, piece, ((0,), (0,)))
        part[...] = total

    f2(0)
    f2(1)
    arrived(bundle1(xm, 1), r_x1.at[1])
    arrived(bundle1(xp, 0), r_x1.at[3])
    share1(xm, 1)
    share1(xp, 0)
    y_step(3, bundle0, r_y0, share0)
    f2(2)
    y_step(4, bundle0, r_y0, share0)
    arrived(bundle1(x2, 0), r_x1.at[4])
    arrived(bundle1(x2, 1), r_x1.at[5])
    share1(x2, 0)
    share1(x2, 1)
    f2(3)

    for k in range(8):
        arrived(ag0.at[1 - c, k], r_s0.at[k])
    for k in range(4):
        for half in range(2):
            arrived(ag1.at[1 - c, k, pl.ds(4 * half, 4)], r_s1.at[2 * k + half])

    def prepare(i):
        xs = div(i, 4)
        m = rem(i, 4)
        lanes = pl.ds(pl.multiple_of(128 * m, 128), 128)
        for h in range(2):
            for ref, at, size in ((ag0, 0, U0), (ag1, U0, U1)):
                if at == 0:
                    t0, t1 = ref[h, 2 * m, xs], ref[h, 2 * m + 1, xs]
                else:
                    t0, t1 = ref[h, xs, 2 * m], ref[h, xs, 2 * m + 1]
                low = lax.broadcasted_iota(jnp.int32, (size, 128), 1) < 64
                for side, value in (
                    (0, jnp.where(low, t0, pltpu.roll(t1, 64, 1))),
                    (4, jnp.where(low, pltpu.roll(t0, 64, 1), t1)),
                ):
                    high, rest = split(value)
                    rows = slice(HALF * h + at, HALF * h + at + size)
                    ah[xs + side, rows, lanes] = high
                    al[xs + side, rows, lanes] = rest

    def prepare_range(lo, hi):
        def body(i, carry):
            prepare(i)
            return carry

        lax.fori_loop(lo, hi, body, 0)

    prepare_range(0, 8)
    f3(0)
    prepare_range(8, 16)
    f3(1)

    def product(t, s):
        near = jnp.where(t == 0, 0, jnp.where(t == 1, -2, jnp.where(t == 2, 2, 4)))
        odd = jnp.where(t == 0, -1, jnp.where(t == 1, 1, jnp.where(t == 2, -3, 3)))
        j = 2 * div(zz(jnp.where(eq, near, odd)), 2) + s
        keep = lax.broadcasted_iota(jnp.int32, (64, B), 0) < 60
        for k in range(8):
            value = jnp.where(keep, fg[j, 60 * k : 60 * k + 64, :], 0.0)
            high, rest = split(value)
            fph[64 * k : 64 * k + 64, :] = high
            fpl[64 * k : 64 * k + 64, :] = rest
        acc[...] += dot3((ah[j], al[j]), (fph[...], fpl[...]), ((1,), (0,)))

    def products(lo, hi):
        def body(i, carry):
            product(div(i, 2), rem(i, 2))
            return carry

        lax.fori_loop(2 * lo, 2 * hi, body, 0)

    @pl.when(eq)
    def _():
        for q in range(2):
            f_wait(z, 1 - c, q)

    products(0, 1)
    f3(2)
    products(1, 2)
    f3(3)
    products(2, 3)

    @pl.when(eq)
    def _():
        for e in range(4):
            f_wait(zz(4), e % 2, e // 2)

    products(3, 4)

    @pl.when(ne)
    def _():
        go(acc, cr, r_c.at[0], dev(x, y, 2 * zh + c, a), "ne")

    part[...] += dot3(split(fg[2 * zh + a, 0:SLAB, :]), split(acc[...]), ((0,), (0,)))

    apart = jnp.where(eq, 0, 1)

    def give(k, core, kind):
        owner = zz(2 * k + apart)
        rows = pl.ds(pl.multiple_of(32 * (2 * div(owner, 2) + core), 32), 32)
        go(part.at[rows, :], dr.at[z], r_d.at[z], dev(x, y, owner, core), kind)

    for k in (2, 1, 3):
        give(k, c, "all")
        give(k, 1 - c, "all")
    give(0, 1 - c, "all")

    @pl.when(ne)
    def _():
        give(0, c, "ne")

    @pl.when(eq)
    def _():
        dr[z] = part[pl.ds(pl.multiple_of(32 * p, 32), 32), :]
        sel_ref[...] = -masked(acc[...])

    @pl.when(ne)
    def _():
        arrived(cr, r_c.at[0])
        sel_ref[...] = -masked(cr[...])
        arrived(dr.at[z], r_d.at[z])

    for k in range(1, 8):
        arrived(dr.at[zz(k)], r_d.at[zz(k)])
    total = dr[0]
    for k in range(1, 8):
        total = total + dr[k]
    diag_ref[0] = total

    def finish(kind):
        like = {
            (HALF, B): fu.at[pl.ds(0, HALF), :],
            (120, 128): pk.at[0],
            (U0, 128): ag0.at[0, 0, 0],
            (U1, 128): ag1.at[0, 0, 0],
            (4, U0, 128): ag0.at[0, 0],
            (4, U1, 128): ag1.at[0, 0, pl.ds(0, 4)],
            (SLAB, B): acc,
            (32, B): lb.at[0],
        }
        for shape, index in pending[kind]:
            pltpu.make_async_remote_copy(
                src_ref=like[shape], dst_ref=like[shape], send_sem=send.at[index], recv_sem=r_l.at[0],
                device_id=sibling, device_id_type=MESH,
            ).wait_send()

    finish("all")

    @pl.when(eq)
    def _():
        finish("eq")

    @pl.when(ne)
    def _():
        finish("ne")


def on_device(ancestor_inverse, factor, struct_rows, diag_factor_inverse):
    vmem = pl.BlockSpec(memory_space=pltpu.VMEM)
    dma = pltpu.SemaphoreType.DMA
    return pl.pallas_call(
        kernel,
        out_shape=(
            jax.ShapeDtypeStruct((SLAB, B), F32),
            jax.ShapeDtypeStruct((1, 32, B), F32),
        ),
        in_specs=[vmem, vmem, pl.BlockSpec(memory_space=pltpu.SMEM), vmem],
        out_specs=(vmem, vmem),
        scratch_shapes=[
            pltpu.VMEM((SLAB, 128), F32),
            pltpu.VMEM((2, 120, 128), F32),
            pltpu.VMEM((2, 120, 128), F32),
            pltpu.VMEM((2, NY, NX, U0, 128), F32),
            pltpu.VMEM((2, NX, NY, U1, 128), F32),
            pltpu.VMEM((8, SLAB, 512), BF16),
            pltpu.VMEM((8, SLAB, 512), BF16),
            pltpu.VMEM((SLAB, B), F32),
            pltpu.VMEM((8, SLAB + 8, B), F32),
            pltpu.VMEM((512, B), BF16),
            pltpu.VMEM((512, B), BF16),
            pltpu.VMEM((SLAB, B), F32),
            pltpu.VMEM((SLAB, B), F32),
            pltpu.VMEM((2, 32, B), F32),
            pltpu.VMEM((B, B), F32),
            pltpu.VMEM((8, 32, B), F32),
            dma((96,)),
            dma((2,)),
            dma((3,)),
            dma((7,)),
            dma((7,)),
            dma((6,)),
            dma((8,)),
            dma((8,)),
            dma((16,)),
            dma((1,)),
            dma((1,)),
            dma((8,)),
        ],
        compiler_params=pltpu.CompilerParams(
            collective_id=0, has_side_effects=True, vmem_limit_bytes=48 * 1024 * 1024
        ),
    )(ancestor_inverse, factor, struct_rows, diag_factor_inverse)


def solution(mesh):
    placed = (P("pcol", "prow"), P("pcol", "prow"), P("prow", None), P("prow", "pcol", None))
    return jax.shard_map(
        on_device,
        mesh=mesh,
        in_specs=placed,
        out_specs=(P("pcol", "prow"), P("prow", "pcol", None)),
        check_vma=False,
    )
```

time: 447 us -> 85.9 us (0.19)
  waiting for transfers between devices: 401 us -> 0 us
  Pallas kernels: 0 us -> 81.6 us
  matrix products: 19.1 us -> 0 us
  between operations: 13.8 us -> 0.69 us
  local copies, waits for them, and re-layouts: 8.59 us -> 3.47 us
    all_gather x2 -> x0, waiting for transfers between devices: 364 us -> none  [the longest x1 281 us: on_device(): lax.all_gather(ancestor_inverse, 'prow', axis=1, tiled=True)]
    pallas_call x0 -> x1, Pallas kernels: none -> 81.6 us  [on_device(): pl.pallas_call(kernel, out_shape=(jax.ShapeDtypeStruct((SLAB, B), F32), j...]
    reduce_scatter x1 -> x0, waiting for transfers between devices: 36 us -> none  [on_device(): lax.psum_scatter(gram_part - inner_part, 'pcol', scatter_dimension=1, til...]
    dot_general x3 -> x0, matrix products: 19.1 us -> none  [the longest x1 16.1 us: on_device(): jnp.dot(lax.all_gather(ancestor_inverse, 'prow', axis=1, tiled=True), ful...]
    unnamed x5 -> x9, local copies, waits for them, and re-layouts: 8.59 us -> 3.47 us
  transfers between devices with their start and end apart: 3 -> 0, of which waited for: 3 -> 0; matrix products, arithmetic and copies ran while one was open for 3% -> 0% of each run, Pallas kernels for 0% -> 0%
where the time goes in v1:
time: 85.9 us; the launch traced here: 85.7 us
  Pallas kernels  81.6 us (95%)
  local copies, waits for them, and re-layouts  3.47 us (4%)
    pallas_call x1, Pallas kernels, on_device(): pl.pallas_call(kernel, out_shape=(jax.ShapeDtypeStruct((SLAB, B), F32), j...  81.6 us
    unnamed x9, local copies, waits for them, and re-layouts  3.47 us

profile of v1, /device:TPU:1, one launch (start us, length us, event | category | flops | bytes accessed | tf_op | source)
XLA Modules:
  0.0 85.7 jit_solution(12478840886436954196)
XLA Ops:
  0.6 0.0 copy-start.1
  0.6 0.0 copy-start.2
  0.6 1.0 %copy.6.a_ref = f32[480,60]{1,0:T(8,128)S(1)} copy(f32[480,60]{0,1:T(8,128)} %param.4) | data formatting | bytes 230400 | tf_op args[0]
  1.7 0.0 copy-done.1
  1.7 0.0 copy-done.2
  1.7 0.0 copy-start
  1.7 1.0 %copy-done = f32[480,256]{1,0:T(8,128)S(1)} copy-done((f32[480,256]{1,0:T(8,128)S(1)}, f32[480,256]{1,0:T(8,128)}, u32[]{:S(2)}) %copy-start) | copy-done | bytes 491544
  2.8 81.6 %shard_map.59 = (f32[480,256]{1,0:T(8,128)S(1)}, f32[1,32,256]{2,1,0:T(8,128)S(1)}) custom-call(f32[480,60]{1,0:T(8,128)S(1)} %copy.6.a_ref, f32[480,256]{1,0:T(8,128)S(1)} %copy-done, s32[1,11]{1,0:T(1,128)S(1)} %copy-done.2, f32[1,32,256]{2,1,0:T(8,128)S(1)} %copy-done.1), custom_call_target="tpu_custom_call" | custom-call | tf_op jit(solution)/shard_map/pallas_call | solution.py:433
  84.3 0.8 copy.9
  85.1 0.6 copy.10
Async XLA Ops:
  0.6 1.1 %copy-start.1 = (f32[1,32,256]{2,1,0:T(8,128)S(1)}, f32[1,32,256]{2,1,0:T(8,128)}, u32[]{:S(2)}) copy-start(f32[1,32,256]{2,1,0:T(8,128)} %d_ref.1) | copy-start | bytes 98308
  0.6 1.1 %copy-start.2 = (s32[1,11]{1,0:T(1,128)S(1)}, s32[1,11]{1,0:T(1,128)}, u32[]{:S(2)}) copy-start(s32[1,11]{1,0:T(1,128)} %s_ref.1) | copy-start | bytes 136
  1.7 1.0 %copy-start = (f32[480,256]{1,0:T(8,128)S(1)}, f32[480,256]{1,0:T(8,128)}, u32[]{:S(2)}) copy-start(f32[480,256]{1,0:T(8,128)} %f_ref.1) | copy-start | bytes 1474564

commit v2 on v1

v2 whole, which is shorter than its diff:
```python
import jax
import jax.numpy as jnp
import numpy as np
from jax import lax
from jax.experimental import pallas as pl
from jax.experimental.pallas import tpu as pltpu
from jax.sharding import PartitionSpec as P

MESH = pl.DeviceIdType.MESH
F32 = jnp.float32
BF16 = jnp.bfloat16
NX, NY, NZ = 4, 8, 8
B = 256
SLAB = 480
HALF = 240
U0 = 64
U1 = 176
NQ = 4
CHUNK = SLAB // NQ
MOST = 5
EQ_FIRST = (
    ("own",), ("y1", -1), ("y1", 1), ("x0",), ("xp", 1), ("xp", 0), ("y1", -2), ("y1", 2), ("gram",),
    ("y0", 1, -1, 0), ("y0", 1, 1, 0), ("y0", 1, -1, 1), ("y1", -3), ("y0", 2, 1, 0), ("y0", 2, -1, 0),
    ("y0", 1, 1, 1), ("y1", 4), ("y1", 3), ("y0", 2, 1, 1), ("f2", 2, -1), ("y0", 3, -1, 0), ("y0", 3, 1, 0),
    ("xp", 2), ("f2", 0, -1), ("xp", 4), ("f2", 2, 1), ("f2", 0, 1), ("xp", 3), ("f2", 1, -1), ("y0", 2, -1, 1),
    ("sh", 0), ("xp", -1), ("f2", 5, -1), ("y0", 3, 1, 1), ("xp", -2), ("f2", 1, 1), ("xp", -3), ("f2", 4, -1),
    ("f2", 6, 1), ("f2", 4, 1), ("f2", 7, 1), ("f2", 3, 1), ("f2", 3, -1), ("f2", 5, 1), ("sh", 2), ("f2", 6, -1),
    ("sh", 1), ("y0", 3, -1, 1), ("y0", 4, 1, 0), ("f2", 7, -1), ("sh", 3), ("y0", 4, 1, 1),
)
NE_FIRST = (
    ("f1", 0, 1), ("a0",), ("y1", -1), ("x0",), ("f1", 2, 1), ("f1", 1, -1), ("y0", 1, 1, 0), ("y1", 1), ("f1", 3, 1),
    ("f1", 0, -1), ("y1", 2), ("y1", -2), ("f1", 5, 1), ("f1", 1, 1), ("f1", 2, -1), ("y0", 1, -1, 0), ("f1", 5, -1),
    ("f1", 3, -1), ("f1", 6, -1), ("y0", 1, 1, 1), ("y1", 3), ("f1", 7, -1), ("f1", 4, 1), ("y0", 1, -1, 1),
    ("f1", 6, 1), ("y0", 2, 1, 0), ("y1", -3), ("f1", 4, -1), ("y0", 2, -1, 0), ("f1", 7, 1), ("y1", 4), ("xp", 1),
    ("xp", 2), ("y0", 2, 1, 1), ("sh", 0), ("y0", 3, 1, 0), ("xp", 0), ("xp", -1), ("xp", 3), ("xp", -3),
    ("y0", 2, -1, 1), ("xp", -2), ("xp", 4), ("sh", 2), ("y0", 3, 1, 1), ("sh", 1), ("y0", 3, -1, 1),
    ("y0", 3, -1, 0), ("y0", 4, 1, 0), ("f3", 0), ("sh", 3), ("y0", 4, 1, 1), ("f3", 2),
)
NE_LATER = (
    (("f3", 1),),
    (),
    (),
    (("f3", 5), ("f3", 4), ("f3", 7), ("f3", 6), ("f3", 3), ("fr", 0), ("fr", 1), ("fr", 2), ("fr", 3), ("fr", 4), ("fr", 5), ("fr", 6), ("fr", 7)),
)


def split(v):
    high = v.astype(BF16)
    return high, (v - high.astype(F32)).astype(BF16)


def dot3(left, right, dims):
    lh, ll = left
    rh, rl = right
    go = lambda p, q: lax.dot_general(p, q, (dims, ((), ())), preferred_element_type=F32)
    return go(lh, rh) + (go(ll, rh) + go(lh, rl))


def kernel(
    a_ref, f_ref, s_ref, d_ref, sel_ref, diag_ref,
    ta, tw, tz, pk, ag0, ag1, ah, al, fu, fg, fph, fpl, acc, cr, lb, part, pr, dr,
    local, send, r_a0, r_x0, r_y1, r_y0, r_x1, r_s0, r_s1, r_f, r_l, r_c, r_p, r_d,
):
    def rem(value, by):
        return lax.rem(value, np.int32(by))

    def div(value, by):
        return lax.div(value, np.int32(by))

    r, p = lax.axis_index("prow"), lax.axis_index("pcol")
    a, x, y = div(r, 32), rem(div(r, 8), 4), rem(r, 8)
    zh, c = div(p, 2), rem(p, 2)
    z = 2 * zh + a
    eq, ne = a == c, a != c
    dsg = 1 - 2 * c
    xp, xm, x2 = rem(x + 4 + dsg, 4), rem(x + 4 - dsg, 4), rem(x + 2, 4)

    def yy(k):
        return rem(y + 16 + k * dsg, 8)

    def zz(k):
        return rem(z + 8 + k, 8)

    def dev(x_, y_, z_, c_):
        return (rem(z_, 2) * 32 + x_ * 8 + y_, div(z_, 2) * 2 + c_)

    counter = [0]
    pending = {"all": [], "eq": [], "ne": []}

    def go(src, dst, recv, device, kind="all"):
        copy = pltpu.make_async_remote_copy(
            src_ref=src, dst_ref=dst, send_sem=send.at[counter[0]], recv_sem=recv,
            device_id=device, device_id_type=MESH,
        )
        counter[0] += 1
        copy.start()
        pending[kind].append((src.shape, counter[0] - 1))

    sibling = dev(x, y, z, 1 - c)

    def arrived(dst, recv):
        pltpu.make_async_remote_copy(
            src_ref=dst, dst_ref=dst, send_sem=send.at[0], recv_sem=recv,
            device_id=sibling, device_id_type=MESH,
        ).wait_recv()

    loads = [
        pltpu.make_async_copy(a_ref, ta, local.at[0]),
        pltpu.make_async_copy(f_ref, fu, local.at[1]),
        pltpu.make_async_copy(d_ref.at[0], lb.at[0], local.at[2]),
    ]
    for load in loads:
        load.start()
    barrier = pltpu.get_barrier_semaphore()
    greeted = [sibling]
    for k in (1, -1, 2, -2, 4):
        greeted += [dev(x, y, zz(k), 0), dev(x, y, zz(k), 1)]
    greeted += [dev(xp, y, z, c), dev(xm, y, z, c), dev(x2, y, z, c)]
    greeted += [dev(x, yy(k), z, c) for k in (1, -1, 2, -2)]
    for device in greeted:
        pl.semaphore_signal(barrier, inc=1, device_id=device, device_id_type=MESH)

    tw[...] = jnp.zeros_like(tw)
    for load in loads:
        load.wait()
    tw[0:60, 0:SLAB] = ta[...]
    tz[...] = jnp.transpose(tw[...])
    pk[...] = tz[0:HALF, :] + pltpu.roll(tz[HALF:SLAB, :], 64, 1)

    first = div(SLAB * p, B)

    def listed(block):
        total = np.float32(0.0)
        for i in range(s_ref.shape[1]):
            total = jnp.maximum(total, jnp.where(s_ref[0, i] == block, np.float32(1.0), np.float32(0.0)))
        return total

    present = [listed(first + i) for i in range(3)]

    def masked(value):
        block = (lax.broadcasted_iota(jnp.int32, (SLAB, B), 0) + SLAB * p) // B - first
        return value * jnp.where(block == 0, present[0], jnp.where(block == 1, present[1], present[2]))

    fu[...] = masked(fu[...])

    @pl.when(eq)
    def _():
        ag0[c, y, 0] = pk[0:U0, :]
        ag1[c, x, y] = pk[U0:HALF, :]

    row = lax.broadcasted_iota(jnp.int32, (32, B), 0) + 32 * p
    lb[0] = jnp.where(row >= lax.broadcasted_iota(jnp.int32, (32, B), 1), lb[0], 0.0)

    pl.semaphore_wait(barrier, len(greeted))

    @pl.when(ne)
    def _():
        partner = dev(x, y, 2 * zh + c, a)
        go(pk.at[pl.ds(0, U0), :], ag0.at[a, y, 0], r_a0.at[0], partner, "ne")
        go(pk.at[pl.ds(U0, U1), :], ag1.at[a, x, y], r_a0.at[1], partner, "ne")

    def fslot(j, q):
        return fg.at[j, pl.ds(CHUNK * q, CHUNK), :]

    for q in range(NQ):
        for sign in (1, -1):
            go(fu.at[pl.ds(CHUNK * q, CHUNK), :], fslot(p, q), r_f.at[NQ * p + q], dev(x, y, zz(sign), a))

    @pl.when(ne)
    def _():
        for q in range(NQ):
            go(fu.at[pl.ds(CHUNK * q, CHUNK), :], fslot(p, q), r_f.at[NQ * p + q], sibling, "ne")
        go(lb.at[0], lb.at[1], r_l.at[0], sibling, "ne")

    @pl.when(eq)
    def _():
        fg[p, 0:SLAB, :] = fu[...]

    for j in range(8):
        fg[j, SLAB : SLAB + 8, :] = jnp.zeros((8, B), F32)
    acc[...] = jnp.zeros_like(acc)
    part[...] = jnp.zeros_like(part)

    def f_wait(source, s, q):
        j = 2 * div(source, 2) + s
        arrived(fslot(j, q), r_f.at[NQ * j + q])
        return j

    def f_pass(e, distance, sign, kind):
        s, q = e % 2, e // 2
        j = f_wait(zz(-distance * sign), s, q)
        go(fslot(j, q), fslot(j, q), r_f.at[NQ * j + q], dev(x, y, zz(sign), c), kind)

    def f1(e, sign):
        f_pass(e, 1, sign, "ne")

    def f2(e, sign):
        f_pass(e, 2, sign, "eq")

    def f3(e):
        s, q = e % 2, e // 2
        way = dsg if e < MOST else -dsg
        j = f_wait(zz(8 - 3 * way), s, q)
        go(fslot(j, q), fslot(j, q), r_f.at[NQ * j + q], dev(x, y, zz(way), c), "ne")

    def f3_rest(e):
        way = dsg if e < MOST else -dsg
        f_wait(zz(3 * way), e % 2, e // 2)

    to_xp, to_xm, to_x2 = dev(xp, y, z, c), dev(xm, y, z, c), dev(x2, y, z, c)

    def to_y(k):
        return dev(x, yy(k), z, c)

    def tile1(y_):
        return ag1.at[c, x, y_]

    def group0(y_, half):
        return ag0.at[c, y_, pl.ds(3 * half - 2 * half, 1 + 2 * half)]

    def along_x(k):
        src = tile1(yy(k))
        go(src, src, r_x1.at[yy(k)], to_xp, kind[0])
        go(src, src, r_x1.at[8 + yy(k)], to_xm, kind[0])

    def x1_pass(k):
        y_ = yy(k)
        if k in (0, -1, 2, -3):
            src = ag1.at[c, xm, y_]
            arrived(src, r_x1.at[y_])
            go(src, src, r_x1.at[16 + y_], to_xp, kind[0])
        else:
            src = ag1.at[c, xp, y_]
            arrived(src, r_x1.at[8 + y_])
            go(src, src, r_x1.at[16 + y_], to_xm, kind[0])

    def y1_wait(k):
        arrived(tile1(yy(-k)), r_y1.at[k + 3])

    def y1_go(own, k, kind):
        go(tile1(yy(own)), tile1(yy(own)), r_y1.at[k - own + 3], to_y(k), kind)

    def y0_go(k, sign, half):
        src = group0(yy(-sign * (k - 1)), half)
        go(src, src, r_y0.at[2 * (k - 1 + (0 if sign > 0 else 4)) + half], to_y(sign), kind[0])

    kind = ["all"]
    seen = set()

    def share0(y_):
        src = ag0.at[c, y_]
        go(src, src, r_s0.at[y_], sibling, kind[0])

    def share1(x_):
        src = ag1.at[c, x_]
        go(src, src, r_s1.at[x_], sibling, kind[0])

    def own_out():
        for k in (1, -1, 2, -2):
            y1_go(0, k, kind[0])
        src = ag0.at[c, y, 0]
        go(src, ag0.at[c, y, 2 + dsg], r_x0.at[0], to_xp, kind[0])
        go(src, ag0.at[c, y, 2 - dsg], r_x0.at[1], to_xm, kind[0])
        go(src, ag0.at[c, y, 2], r_x0.at[2], to_x2, kind[0])
        along_x(0)
        for sign in (1, -1):
            y0_go(1, sign, 0)

    def do_a0():
        arrived(ag0.at[c, y, 0], r_a0.at[0])
        arrived(ag1.at[c, x, y], r_a0.at[1])
        own_out()

    def do_x0():
        arrived(ag0.at[c, y, 2 + dsg], r_x0.at[0])
        arrived(ag0.at[c, y, 2 - dsg], r_x0.at[1])
        arrived(ag0.at[c, y, 2], r_x0.at[2])
        for sign in (1, -1):
            y0_go(1, sign, 1)
        share0(y)

    def do_y1(k):
        y1_wait(k)
        if k == 2:
            y1_go(-2, 1, kind[0])
            y1_go(-2, 2, kind[0])
        if k == -2:
            y1_go(2, -1, kind[0])
        along_x(4 if k == 4 else -k)

    def do_y0(k, sign, half):
        arrived(group0(yy(-sign * k), half), r_y0.at[2 * (k - 1 + (0 if sign > 0 else 4)) + half])
        if k < (4 if sign > 0 else 3):
            y0_go(k + 1, sign, half)
        if (k, sign) in seen:
            share0(yy(-sign * k))
        seen.add((k, sign))

    FROM_M = (0, -1, 2, -3)
    TILES = (0, 1, -1, 2, -2, 3, -3, 4)

    def do_share(which):
        if which == 0:
            share1(x)
        elif which == 1:
            for k in TILES:
                if k not in FROM_M:
                    arrived(ag1.at[c, xm, yy(k)], r_x1.at[yy(k)])
            share1(xm)
        elif which == 2:
            for k in TILES:
                if k in FROM_M:
                    arrived(ag1.at[c, xp, yy(k)], r_x1.at[8 + yy(k)])
            share1(xp)
        else:
            for k in TILES:
                arrived(ag1.at[c, x2, yy(k)], r_x1.at[16 + yy(k)])
            share1(x2)

    def gram():
        arrived(lb.at[1], r_l.at[0])
        total = jnp.zeros((B, B), F32)
        for i in range(2):
            piece = split(lb[i])
            total = total + dot3(piece, piece, ((0,), (0,)))
        part[...] = total

    steps = {
        "own": own_out, "a0": do_a0, "x0": do_x0, "y1": do_y1, "y0": do_y0, "xp": x1_pass, "sh": do_share,
        "f1": f1, "f2": f2, "f3": f3, "fr": f3_rest, "gram": gram,
    }

    def run(which, order):
        kind[0] = which
        seen.clear()
        for step in order:
            steps[step[0]](*step[1:])

    def both(order_eq, order_ne):
        @pl.when(eq)
        def _():
            run("eq", order_eq)

        @pl.when(ne)
        def _():
            run("ne", order_ne)

    both(EQ_FIRST, NE_FIRST)

    for k in range(8):
        arrived(ag0.at[1 - c, k], r_s0.at[k])
    for k in range(4):
        arrived(ag1.at[1 - c, k], r_s1.at[k])

    def prepare(i):
        xs = div(i, 4)
        m = rem(i, 4)
        lanes = pl.ds(pl.multiple_of(128 * m, 128), 128)
        for side in range(2):
            for ref, at, size in ((ag0, 0, U0), (ag1, U0, U1)):
                if ref is ag0:
                    t0, t1 = ref[side, 2 * m, rem(xs - x + 4, 4)], ref[side, 2 * m + 1, rem(xs - x + 4, 4)]
                else:
                    t0, t1 = ref[side, xs, 2 * m], ref[side, xs, 2 * m + 1]
                low = lax.broadcasted_iota(jnp.int32, (size, 128), 1) < 64
                for top, value in (
                    (at, jnp.where(low, t0, pltpu.roll(t1, 64, 1))),
                    (HALF + at, jnp.where(low, pltpu.roll(t0, 64, 1), t1)),
                ):
                    high, rest = split(value)
                    ah[xs + 4 * side, top : top + size, lanes] = high
                    al[xs + 4 * side, top : top + size, lanes] = rest

    def prepare_range(lo, hi):
        def body(i, carry):
            prepare(i)
            return carry

        lax.fori_loop(lo, hi, body, 0)

    prepare_range(0, 8)
    both((), NE_LATER[0])
    prepare_range(8, 16)
    both((), NE_LATER[1])

    def product(t, s):
        near = jnp.where(t == 0, 0, jnp.where(t == 1, -2, jnp.where(t == 2, 2, 4)))
        odd = jnp.where(t == 0, -1, jnp.where(t == 1, 1, jnp.where(t == 2, -3, 3)))
        j = 2 * div(zz(jnp.where(eq, near, odd)), 2) + s
        keep = lax.broadcasted_iota(jnp.int32, (64, B), 0) < 60
        for k in range(8):
            value = jnp.where(keep, fg[j, 60 * k : 60 * k + 64, :], 0.0)
            high, rest = split(value)
            fph[64 * k : 64 * k + 64, :] = high
            fpl[64 * k : 64 * k + 64, :] = rest
        acc[...] += dot3((ah[j], al[j]), (fph[...], fpl[...]), ((1,), (0,)))

    def products(lo, hi):
        def body(i, carry):
            product(div(i, 2), rem(i, 2))
            return carry

        lax.fori_loop(lo, hi, body, 0)

    @pl.when(eq)
    def _():
        for q in range(NQ):
            f_wait(z, 1 - c, q)

    products(0, 2)
    both((), NE_LATER[2])
    products(2, 4)
    both((), NE_LATER[3])
    products(4, 6)
    for s in range(2):
        @pl.when(eq)
        def _():
            for q in range(NQ):
                f_wait(zz(4), s, q)

        products(6 + s, 7 + s)

    @pl.when(ne)
    def _():
        go(acc, cr, r_c.at[0], dev(x, y, 2 * zh + c, a), "ne")

    part[...] += dot3(split(fg[2 * zh + a, 0:SLAB, :]), split(acc[...]), ((0,), (0,)))

    @pl.when(ne)
    def _():
        go(part, pr, r_p.at[0], dev(x, y, zz(2 * a - 1), c), "ne")

    def give(k, core):
        owner = zz(2 * k)
        rows = pl.ds(pl.multiple_of(32 * (2 * div(owner, 2) + core), 32), 32)
        go(part.at[rows, :], dr.at[zh], r_d.at[zh], dev(x, y, owner, core), "eq")

    @pl.when(eq)
    def _():
        arrived(pr, r_p.at[0])
        part[...] += pr[...]
        for k in (2, 1, 3):
            give(k, c)
            give(k, 1 - c)
        give(0, 1 - c)

    @pl.when(eq)
    def _():
        dr[zh] = part[pl.ds(pl.multiple_of(32 * p, 32), 32), :]
        sel_ref[...] = -masked(acc[...])

    @pl.when(ne)
    def _():
        arrived(cr, r_c.at[0])
        sel_ref[...] = -masked(cr[...])
        arrived(dr.at[zh], r_d.at[zh])

    for k in range(1, 4):
        arrived(dr.at[rem(zh + k, 4)], r_d.at[rem(zh + k, 4)])
    total = dr[0]
    for k in range(1, 4):
        total = total + dr[k]
    diag_ref[0] = total

    def finish(kind):
        like = {
            (CHUNK, B): fu.at[pl.ds(0, CHUNK), :],
            (U0, 128): ag0.at[0, 0, 0],
            (U1, 128): ag1.at[0, 0, 0],
            (1, U0, 128): ag0.at[0, 0, pl.ds(0, 1)],
            (3, U0, 128): ag0.at[0, 0, pl.ds(0, 3)],
            (B, B): part,
            (4, U0, 128): ag0.at[0, 0],
            (8, U1, 128): ag1.at[0, 0],
            (SLAB, B): acc,
            (32, B): lb.at[0],
        }
        for shape, index in pending[kind]:
            pltpu.make_async_remote_copy(
                src_ref=like[shape], dst_ref=like[shape], send_sem=send.at[index], recv_sem=r_l.at[0],
                device_id=sibling, device_id_type=MESH,
            ).wait_send()

    finish("all")

    @pl.when(eq)
    def _():
        finish("eq")

    @pl.when(ne)
    def _():
        finish("ne")


def on_device(ancestor_inverse, factor, struct_rows, diag_factor_inverse):
    vmem = pl.BlockSpec(memory_space=pltpu.VMEM)
    anywhere = pl.BlockSpec(memory_space=pl.ANY)
    dma = pltpu.SemaphoreType.DMA
    return pl.pallas_call(
        kernel,
        out_shape=(
            jax.ShapeDtypeStruct((SLAB, B), F32),
            jax.ShapeDtypeStruct((1, 32, B), F32),
        ),
        in_specs=[anywhere, anywhere, pl.BlockSpec(memory_space=pltpu.SMEM), anywhere],
        out_specs=(vmem, vmem),
        scratch_shapes=[
            pltpu.VMEM((60, SLAB), F32),
            pltpu.VMEM((128, 512), F32),
            pltpu.VMEM((512, 128), F32),
            pltpu.VMEM((HALF, 128), F32),
            pltpu.VMEM((2, NY, NX, U0, 128), F32),
            pltpu.VMEM((2, NX, NY, U1, 128), F32),
            pltpu.VMEM((8, SLAB, 512), BF16),
            pltpu.VMEM((8, SLAB, 512), BF16),
            pltpu.VMEM((SLAB, B), F32),
            pltpu.VMEM((8, SLAB + 8, B), F32),
            pltpu.VMEM((512, B), BF16),
            pltpu.VMEM((512, B), BF16),
            pltpu.VMEM((SLAB, B), F32),
            pltpu.VMEM((SLAB, B), F32),
            pltpu.VMEM((2, 32, B), F32),
            pltpu.VMEM((B, B), F32),
            pltpu.VMEM((B, B), F32),
            pltpu.VMEM((4, 32, B), F32),
            dma((3,)),
            dma((256,)),
            dma((2,)),
            dma((3,)),
            dma((8,)),
            dma((14,)),
            dma((24,)),
            dma((8,)),
            dma((4,)),
            dma((8 * NQ,)),
            dma((1,)),
            dma((1,)),
            dma((1,)),
            dma((4,)),
        ],
        compiler_params=pltpu.CompilerParams(
            collective_id=0, has_side_effects=True, vmem_limit_bytes=60 * 1024 * 1024
        ),
    )(ancestor_inverse.T, factor, struct_rows, diag_factor_inverse)


def solution(mesh):
    placed = (P("pcol", "prow"), P("pcol", "prow"), P("prow", None), P("prow", "pcol", None))
    return jax.shard_map(
        on_device,
        mesh=mesh,
        in_specs=placed,
        out_specs=(P("pcol", "prow"), P("prow", "pcol", None)),
        check_vma=False,
    )
```

time: 85.9 us -> 77 us (0.90)
  Pallas kernels: 81.6 us -> 73.8 us
  local copies, waits for them, and re-layouts: 3.47 us -> 2.46 us
    pallas_call x1, Pallas kernels: 81.6 us -> 73.8 us  [on_device(): pl.pallas_call(kernel, out_shape=(jax.ShapeDtypeStruct((SLAB, B), F32), j...]
    unnamed x9 -> x4, local copies, waits for them, and re-layouts: 3.47 us -> 2.46 us
where the time goes in v2:
time: 77 us; the launch traced here: 76.9 us
  Pallas kernels  73.8 us (96%)
  local copies, waits for them, and re-layouts  2.46 us (3%)
    pallas_call x1, Pallas kernels, on_device(): pl.pallas_call(kernel, out_shape=(jax.ShapeDtypeStruct((SLAB, B), F32), j...  73.8 us
    unnamed x4, local copies, waits for them, and re-layouts  2.46 us

profile of v2, /device:TPU:1, one launch (start us, length us, event | category | flops | bytes accessed | tf_op | source)
XLA Modules:
  0.0 76.9 jit_solution(5105293567430460406)
XLA Ops:
  0.6 73.8 %shard_map.59 = (f32[480,256]{1,0:T(8,128)}, f32[1,32,256]{2,1,0:T(8,128)}) custom-call(f32[60,480]{1,0:T(8,128)} %bitcast.1, f32[480,256]{1,0:T(8,128)} %f_ref.1, s32[1,11]{1,0:T(1,128)} %s_ref.1, f32[1,32,256]{2,1,0:T(8,128)} %d_ref.1), custom_call_target="tpu_custom_call" | custom-call | tf_op jit(solution)/shard_map/pallas_call | solution.py:499
  74.4 0.0 copy-start
  74.4 1.8 %copy.8 = f32[480,256]{1,0:T(8,128)} copy(f32[480,256]{1,0:T(8,128)} %get-tuple-element.4) | data formatting | bytes 983040
  76.3 0.0 copy-done
  76.3 0.6 copy.9
Async XLA Ops:
  74.4 1.9 %copy-start = (f32[1,32,256]{2,1,0:T(8,128)S(1)}, f32[1,32,256]{2,1,0:T(8,128)}, u32[]{:S(2)}) copy-start(f32[1,32,256]{2,1,0:T(8,128)} %get-tuple-element.5) | copy-start | bytes 98308

commit v3 on v2

--- a/solution.py
+++ b/solution.py
@@ -58,7 +58,7 @@
 
 def kernel(
     a_ref, f_ref, s_ref, d_ref, sel_ref, diag_ref,
-    ta, tw, tz, pk, ag0, ag1, ah, al, fu, fg, fph, fpl, acc, cr, lb, part, pr, dr,
+    sel_v, diag_v, ta, tw, tz, pk, ag0, ag1, ah, al, fu, fg, fph, fpl, acc, cr, lb, part, pr, dr,
     local, send, r_a0, r_x0, r_y1, r_y0, r_x1, r_s0, r_s1, r_f, r_l, r_c, r_p, r_d,
 ):
     def rem(value, by):
@@ -113,7 +113,7 @@
         load.start()
     barrier = pltpu.get_barrier_semaphore()
     greeted = [sibling]
-    for k in (1, -1, 2, -2, 4):
+    for k in (1, -1):
         greeted += [dev(x, y, zz(k), 0), dev(x, y, zz(k), 1)]
     greeted += [dev(xp, y, z, c), dev(xm, y, z, c), dev(x2, y, z, c)]
     greeted += [dev(x, yy(k), z, c) for k in (1, -1, 2, -2)]
@@ -447,12 +447,18 @@
     @pl.when(eq)
     def _():
         dr[zh] = part[pl.ds(pl.multiple_of(32 * p, 32), 32), :]
-        sel_ref[...] = -masked(acc[...])
+        sel_v[...] = -masked(acc[...])
 
     @pl.when(ne)
     def _():
         arrived(cr, r_c.at[0])
-        sel_ref[...] = -masked(cr[...])
+        sel_v[...] = -masked(cr[...])
+
+    sel_out = pltpu.make_async_copy(sel_v, sel_ref, local.at[0])
+    sel_out.start()
+
+    @pl.when(ne)
+    def _():
         arrived(dr.at[zh], r_d.at[zh])
 
     for k in range(1, 4):
@@ -460,7 +466,9 @@
     total = dr[0]
     for k in range(1, 4):
         total = total + dr[k]
-    diag_ref[0] = total
+    diag_v[...] = total
+    diag_out = pltpu.make_async_copy(diag_v, diag_ref.at[0], local.at[1])
+    diag_out.start()
 
     def finish(kind):
         like = {
@@ -491,20 +499,28 @@
     def _():
         finish("ne")
 
+    sel_out.wait()
+    diag_out.wait()
+
+
+def hand_over(sel_ref, diag_ref, sel_out, diag_out):
+    sel_out[...] = sel_ref[...]
+    diag_out[...] = diag_ref[...]
+
 
 def on_device(ancestor_inverse, factor, struct_rows, diag_factor_inverse):
     vmem = pl.BlockSpec(memory_space=pltpu.VMEM)
     anywhere = pl.BlockSpec(memory_space=pl.ANY)
     dma = pltpu.SemaphoreType.DMA
-    return pl.pallas_call(
+    shapes = (jax.ShapeDtypeStruct((SLAB, B), F32), jax.ShapeDtypeStruct((1, 32, B), F32))
+    results = pl.pallas_call(
         kernel,
-        out_shape=(
-            jax.ShapeDtypeStruct((SLAB, B), F32),
-            jax.ShapeDtypeStruct((1, 32, B), F32),
-        ),
+        out_shape=shapes,
         in_specs=[anywhere, anywhere, pl.BlockSpec(memory_space=pltpu.SMEM), anywhere],
-        out_specs=(vmem, vmem),
+        out_specs=(anywhere, anywhere),
         scratch_shapes=[
+            pltpu.VMEM((SLAB, B), F32),
+            pltpu.VMEM((32, B), F32),
             pltpu.VMEM((60, SLAB), F32),
             pltpu.VMEM((128, 512), F32),
             pltpu.VMEM((512, 128), F32),
@@ -542,6 +558,12 @@
             collective_id=0, has_side_effects=True, vmem_limit_bytes=60 * 1024 * 1024
         ),
     )(ancestor_inverse.T, factor, struct_rows, diag_factor_inverse)
+    return pl.pallas_call(
+        hand_over,
+        out_shape=shapes,
+        in_specs=[vmem, vmem],
+        out_specs=(vmem, vmem),
+    )(*results)
 
 
 def solution(mesh):

time: 77 us -> 74.3 us (0.965)
  local copies, waits for them, and re-layouts: 2.46 us -> 0 us
    unnamed x4 -> x0, local copies, waits for them, and re-layouts: 2.46 us -> none
    pallas_call x1 -> x2, Pallas kernels: 73.8 us -> 73.5 us  [the longest x1 71.7 us: on_device(): pl.pallas_call(kernel, out_shape=shapes, in_specs=[anywhere, anywhere, pl...]
where the time goes in v3:
time: 74.3 us; the launch traced here: 74.1 us
  Pallas kernels  73.5 us (99%)
    pallas_call x1, Pallas kernels, on_device(): pl.pallas_call(kernel, out_shape=shapes, in_specs=[anywhere, anywhere, pl...  71.7 us
    pallas_call x1, Pallas kernels, on_device(): pl.pallas_call(hand_over, out_shape=shapes, in_specs=[vmem, vmem], out_sp...  1.85 us

profile of v3, /device:TPU:1, one launch (start us, length us, event | category | flops | bytes accessed | tf_op | source)
XLA Modules:
  0.0 74.1 jit_solution(9704800767540195956)
XLA Ops:
  0.6 71.7 %shard_map.59 = (f32[480,256]{1,0:T(8,128)}, f32[1,32,256]{2,1,0:T(8,128)}) custom-call(f32[60,480]{1,0:T(8,128)} %bitcast.1, f32[480,256]{1,0:T(8,128)} %f_ref.1, s32[1,11]{1,0:T(1,128)} %s_ref.1, f32[1,32,256]{2,1,0:T(8,128)} %d_ref.1), custom_call_target="tpu_custom_call" | custom-call | tf_op jit(solution)/shard_map/pallas_call | solution.py:516
  72.3 1.8 %shard_map.60 = (f32[480,256]{1,0:T(8,128)}, f32[1,32,256]{2,1,0:T(8,128)}) custom-call(f32[480,256]{1,0:T(8,128)} %get-tuple-element.4.sel_ref, f32[1,32,256]{2,1,0:T(8,128)} %get-tuple-element.5.diag_ref), custom_call_target="tpu_custom_call" | custom-call | tf_op jit(solution)/shard_map/pallas_call | solution.py:561

commit v4 on v3

--- a/solution.py
+++ b/solution.py
@@ -17,30 +17,31 @@
 U1 = 176
 NQ = 4
 CHUNK = SLAB // NQ
-MOST = 5
+MOST = 4
 EQ_FIRST = (
-    ("own",), ("y1", -1), ("y1", 1), ("x0",), ("xp", 1), ("xp", 0), ("y1", -2), ("y1", 2), ("gram",),
-    ("y0", 1, -1, 0), ("y0", 1, 1, 0), ("y0", 1, -1, 1), ("y1", -3), ("y0", 2, 1, 0), ("y0", 2, -1, 0),
-    ("y0", 1, 1, 1), ("y1", 4), ("y1", 3), ("y0", 2, 1, 1), ("f2", 2, -1), ("y0", 3, -1, 0), ("y0", 3, 1, 0),
-    ("xp", 2), ("f2", 0, -1), ("xp", 4), ("f2", 2, 1), ("f2", 0, 1), ("xp", 3), ("f2", 1, -1), ("y0", 2, -1, 1),
-    ("sh", 0), ("xp", -1), ("f2", 5, -1), ("y0", 3, 1, 1), ("xp", -2), ("f2", 1, 1), ("xp", -3), ("f2", 4, -1),
-    ("f2", 6, 1), ("f2", 4, 1), ("f2", 7, 1), ("f2", 3, 1), ("f2", 3, -1), ("f2", 5, 1), ("sh", 2), ("f2", 6, -1),
-    ("sh", 1), ("y0", 3, -1, 1), ("y0", 4, 1, 0), ("f2", 7, -1), ("sh", 3), ("y0", 4, 1, 1),
+    ("own",), ("y1", 1), ("y1", -1), ("x0",), ("xp", -1), ("y1", -2), ("y1", 2), ("y0", 1, -1, 1), ("gram",),
+    ("y0", 1, 1, 0), ("y0", 1, -1, 0), ("xp", 1), ("y1", -3), ("y1", 4), ("xp", -2), ("y0", 1, 1, 1), ("y0", 2, 1, 0),
+    ("y1", 3), ("f2", 0, 1), ("f2", 0, -1), ("xp", 0), ("f2", 1, 1), ("y0", 2, -1, 1), ("y0", 3, 1, 0),
+    ("y0", 2, -1, 0), ("f2", 1, -1), ("f2", 2, 1), ("y0", 2, 1, 1), ("xp", 2), ("sh", 0), ("xp", 3), ("f2", 2, -1),
+    ("f2", 3, 1), ("y0", 3, -1, 0), ("xp", 4), ("xp", -3), ("f2", 3, -1), ("f2", 4, 1), ("y0", 4, 1, 0),
+    ("f2", 4, -1), ("sh", 2), ("sh", 1), ("y0", 3, 1, 1), ("f2", 5, 1), ("f2", 5, -1), ("f2", 6, 1), ("sh", 3),
+    ("f2", 6, -1), ("y0", 4, 1, 1), ("f2", 7, 1), ("f2", 7, -1), ("y0", 3, -1, 1),
 )
 NE_FIRST = (
-    ("f1", 0, 1), ("a0",), ("y1", -1), ("x0",), ("f1", 2, 1), ("f1", 1, -1), ("y0", 1, 1, 0), ("y1", 1), ("f1", 3, 1),
-    ("f1", 0, -1), ("y1", 2), ("y1", -2), ("f1", 5, 1), ("f1", 1, 1), ("f1", 2, -1), ("y0", 1, -1, 0), ("f1", 5, -1),
-    ("f1", 3, -1), ("f1", 6, -1), ("y0", 1, 1, 1), ("y1", 3), ("f1", 7, -1), ("f1", 4, 1), ("y0", 1, -1, 1),
-    ("f1", 6, 1), ("y0", 2, 1, 0), ("y1", -3), ("f1", 4, -1), ("y0", 2, -1, 0), ("f1", 7, 1), ("y1", 4), ("xp", 1),
-    ("xp", 2), ("y0", 2, 1, 1), ("sh", 0), ("y0", 3, 1, 0), ("xp", 0), ("xp", -1), ("xp", 3), ("xp", -3),
-    ("y0", 2, -1, 1), ("xp", -2), ("xp", 4), ("sh", 2), ("y0", 3, 1, 1), ("sh", 1), ("y0", 3, -1, 1),
-    ("y0", 3, -1, 0), ("y0", 4, 1, 0), ("f3", 0), ("sh", 3), ("y0", 4, 1, 1), ("f3", 2),
+    ("f1", 0, 1), ("a0",), ("y1", 1), ("f1", 0, -1), ("f1", 1, 1), ("f1", 1, -1), ("f1", 2, 1), ("x0",), ("y1", -1),
+    ("f1", 2, -1), ("y1", 2), ("y0", 1, -1, 0), ("f1", 3, 1), ("y0", 1, 1, 0), ("f1", 3, -1), ("y1", -2),
+    ("y0", 1, 1, 1), ("y1", 3), ("f1", 4, 1), ("f1", 4, -1), ("f1", 5, 1), ("y0", 2, -1, 0), ("xp", 0), ("f1", 5, -1),
+    ("y1", -3), ("y0", 2, 1, 0), ("y1", 4), ("f1", 6, 1), ("f1", 6, -1), ("y0", 1, -1, 1), ("f1", 7, 1), ("xp", -2),
+    ("sh", 0), ("xp", -1), ("xp", 2), ("xp", 1), ("y0", 2, 1, 1), ("f1", 7, -1), ("xp", -3), ("y0", 3, 1, 0),
+    ("xp", 3), ("y0", 2, -1, 1), ("xp", 4), ("y0", 3, 1, 1), ("y0", 3, -1, 0), ("sh", 3), ("sh", 1), ("sh", 2),
+    ("y0", 3, -1, 1), ("f3", 0), ("y0", 4, 1, 0), ("y0", 4, 1, 1),
 )
 NE_LATER = (
     (("f3", 1),),
-    (),
-    (),
-    (("f3", 5), ("f3", 4), ("f3", 7), ("f3", 6), ("f3", 3), ("fr", 0), ("fr", 1), ("fr", 2), ("fr", 3), ("fr", 4), ("fr", 5), ("fr", 6), ("fr", 7)),
+    (("f3", 2),),
+    (("f3", 3),),
+    (("f3", 4), ("f3", 5), ("fr", 0), ("fr", 1), ("fr", 2), ("fr", 3)),
+    (("f3", 6), ("f3", 7), ("fr", 4), ("fr", 5), ("fr", 6), ("fr", 7)),
 )
 
 
@@ -58,7 +59,7 @@
 
 def kernel(
     a_ref, f_ref, s_ref, d_ref, sel_ref, diag_ref,
-    sel_v, diag_v, ta, tw, tz, pk, ag0, ag1, ah, al, fu, fg, fph, fpl, acc, cr, lb, part, pr, dr,
+    sel_v, diag_v, ta, tw, tz, pk, ag0, ag1, ah, al, fu, fg, fph, fpl, fth, ftl, acc, cr, lb, part, pr, dr,
     local, send, r_a0, r_x0, r_y1, r_y0, r_x1, r_s0, r_s1, r_f, r_l, r_c, r_p, r_d,
 ):
     def rem(value, by):
@@ -176,8 +177,6 @@
     def _():
         fg[p, 0:SLAB, :] = fu[...]
 
-    for j in range(8):
-        fg[j, SLAB : SLAB + 8, :] = jnp.zeros((8, B), F32)
     acc[...] = jnp.zeros_like(acc)
     part[...] = jnp.zeros_like(part)
 
@@ -383,48 +382,60 @@
     prepare_range(8, 16)
     both((), NE_LATER[1])
 
-    def product(t, s):
+    fth[...], ftl[...] = split(jnp.transpose(fg[2 * zh + a]))
+
+    def product(t, s, h):
         near = jnp.where(t == 0, 0, jnp.where(t == 1, -2, jnp.where(t == 2, 2, 4)))
         odd = jnp.where(t == 0, -1, jnp.where(t == 1, 1, jnp.where(t == 2, -3, 3)))
         j = 2 * div(zz(jnp.where(eq, near, odd)), 2) + s
+        base = pl.multiple_of(HALF * h, 8)
         keep = lax.broadcasted_iota(jnp.int32, (64, B), 0) < 60
-        for k in range(8):
-            value = jnp.where(keep, fg[j, 60 * k : 60 * k + 64, :], 0.0)
-            high, rest = split(value)
+        for k in range(4):
+            value = fg[j, pl.ds(pl.multiple_of(base + 60 * k - 4 * (k % 2), 8), 64), :]
+            if k % 2:
+                value = pltpu.roll(value, 60, 0)
+            high, rest = split(jnp.where(keep, value, 0.0))
             fph[64 * k : 64 * k + 64, :] = high
             fpl[64 * k : 64 * k + 64, :] = rest
-        acc[...] += dot3((ah[j], al[j]), (fph[...], fpl[...]), ((1,), (0,)))
-
-    def products(lo, hi):
+        lanes = pl.ds(pl.multiple_of(256 * h, 256), 256)
+        acc[...] += dot3((ah[j, :, lanes], al[j, :, lanes]), (fph[...], fpl[...]), ((1,), (0,)))
+
+    def products(count, pick):
         def body(i, carry):
-            product(div(i, 2), rem(i, 2))
+            product(*pick(i))
             return carry
 
-        lax.fori_loop(lo, hi, body, 0)
+        lax.fori_loop(0, count, body, 0)
 
     @pl.when(eq)
     def _():
         for q in range(NQ):
             f_wait(z, 1 - c, q)
 
-    products(0, 2)
-    both((), NE_LATER[2])
-    products(2, 4)
-    both((), NE_LATER[3])
-    products(4, 6)
-    for s in range(2):
+    def last_wait(h):
         @pl.when(eq)
         def _():
-            for q in range(NQ):
-                f_wait(zz(4), s, q)
-
-        products(6 + s, 7 + s)
+            for q in range(h * NQ // 2, (h + 1) * NQ // 2):
+                for s in range(2):
+                    f_wait(zz(4), s, q)
+
+    products(4, lambda i: (0, div(i, 2), rem(i, 2)))
+    both((), NE_LATER[2])
+    products(4, lambda i: (1, div(i, 2), rem(i, 2)))
+    both((), NE_LATER[3])
+    products(2, lambda i: (2, i, 0))
+    last_wait(0)
+    products(2, lambda i: (3, i, 0))
+    both((), NE_LATER[4])
+    products(2, lambda i: (2, i, 1))
+    last_wait(1)
+    products(2, lambda i: (3, i, 1))
 
     @pl.when(ne)
     def _():
         go(acc, cr, r_c.at[0], dev(x, y, 2 * zh + c, a), "ne")
 
-    part[...] += dot3(split(fg[2 * zh + a, 0:SLAB, :]), split(acc[...]), ((0,), (0,)))
+    part[...] += dot3((fth[...], ftl[...]), split(acc[...]), ((1,), (0,)))
 
     @pl.when(ne)
     def _():
@@ -530,9 +541,11 @@
             pltpu.VMEM((8, SLAB, 512), BF16),
             pltpu.VMEM((8, SLAB, 512), BF16),
             pltpu.VMEM((SLAB, B), F32),
-            pltpu.VMEM((8, SLAB + 8, B), F32),
-            pltpu.VMEM((512, B), BF16),
-            pltpu.VMEM((512, B), BF16),
+            pltpu.VMEM((8, SLAB, B), F32),
+            pltpu.VMEM((256, B), BF16),
+            pltpu.VMEM((256, B), BF16),
+            pltpu.VMEM((B, SLAB), BF16),
+            pltpu.VMEM((B, SLAB), BF16),
             pltpu.VMEM((SLAB, B), F32),
             pltpu.VMEM((SLAB, B), F32),
             pltpu.VMEM((2, 32, B), F32),

time: 74.3 us -> 73.8 us (level)
  no operation moved by 1% of the time
where the time goes in v4:
time: 73.8 us; the launch traced here: 73.6 us
  Pallas kernels  73 us (99%)
    pallas_call x1, Pallas kernels, on_device(): pl.pallas_call(kernel, out_shape=shapes, in_specs=[anywhere, anywhere, pl...  71.1 us
    pallas_call x1, Pallas kernels, on_device(): pl.pallas_call(hand_over, out_shape=shapes, in_specs=[vmem, vmem], out_sp...  1.85 us

profile of v4, /device:TPU:1, one launch (start us, length us, event | category | flops | bytes accessed | tf_op | source)
XLA Modules:
  0.0 73.6 jit_solution(10134318536096151133)
XLA Ops:
  0.6 71.1 %shard_map.59 = (f32[480,256]{1,0:T(8,128)}, f32[1,32,256]{2,1,0:T(8,128)}) custom-call(f32[60,480]{1,0:T(8,128)} %bitcast.1, f32[480,256]{1,0:T(8,128)} %f_ref.1, s32[1,11]{1,0:T(1,128)} %s_ref.1, f32[1,32,256]{2,1,0:T(8,128)} %d_ref.1), custom_call_target="tpu_custom_call" | custom-call | tf_op jit(solution)/shard_map/pallas_call | solution.py:527
  71.8 1.8 %shard_map.60 = (f32[480,256]{1,0:T(8,128)}, f32[1,32,256]{2,1,0:T(8,128)}) custom-call(f32[480,256]{1,0:T(8,128)} %get-tuple-element.4.sel_ref, f32[1,32,256]{2,1,0:T(8,128)} %get-tuple-element.5.diag_ref), custom_call_target="tpu_custom_call" | custom-call | tf_op jit(solution)/shard_map/pallas_call | solution.py:574

commit v5 on v4

--- a/solution.py
+++ b/solution.py
@@ -59,7 +59,7 @@
 
 def kernel(
     a_ref, f_ref, s_ref, d_ref, sel_ref, diag_ref,
-    sel_v, diag_v, ta, tw, tz, pk, ag0, ag1, ah, al, fu, fg, fph, fpl, fth, ftl, acc, cr, lb, part, pr, dr,
+    sel_v, diag_v, ta, tw, tz, pk, ag0, ag1, ah, al, fu, fg, fph, fpl, fwh, fwl, fth, ftl, acc, cr, lb, part, pr, dr,
     local, send, r_a0, r_x0, r_y1, r_y0, r_x1, r_s0, r_s1, r_f, r_l, r_c, r_p, r_d,
 ):
     def rem(value, by):
@@ -400,6 +400,25 @@
         lanes = pl.ds(pl.multiple_of(256 * h, 256), 256)
         acc[...] += dot3((ah[j, :, lanes], al[j, :, lanes]), (fph[...], fpl[...]), ((1,), (0,)))
 
+    def whole(t):
+        def body(s, carry):
+            near = jnp.where(t == 0, 0, -2)
+            odd = jnp.where(t == 0, -1, 1)
+            j = 2 * div(zz(jnp.where(eq, near, odd)), 2) + s
+            keep = lax.broadcasted_iota(jnp.int32, (64, B), 0) < 60
+            for k in range(8):
+                start = 60 * k - 4 * (k % 2)
+                value = fg[j, start : start + 64, :]
+                if k % 2:
+                    value = pltpu.roll(value, 60, 0)
+                high, rest = split(jnp.where(keep, value, 0.0))
+                fwh[64 * k : 64 * k + 64, :] = high
+                fwl[64 * k : 64 * k + 64, :] = rest
+            acc[...] += dot3((ah[j], al[j]), (fwh[...], fwl[...]), ((1,), (0,)))
+            return carry
+
+        lax.fori_loop(0, 2, body, 0)
+
     def products(count, pick):
         def body(i, carry):
             product(*pick(i))
@@ -419,9 +438,9 @@
                 for s in range(2):
                     f_wait(zz(4), s, q)
 
-    products(4, lambda i: (0, div(i, 2), rem(i, 2)))
+    whole(0)
     both((), NE_LATER[2])
-    products(4, lambda i: (1, div(i, 2), rem(i, 2)))
+    whole(1)
     both((), NE_LATER[3])
     products(2, lambda i: (2, i, 0))
     last_wait(0)
@@ -544,6 +563,8 @@
             pltpu.VMEM((8, SLAB, B), F32),
             pltpu.VMEM((256, B), BF16),
             pltpu.VMEM((256, B), BF16),
+            pltpu.VMEM((512, B), BF16),
+            pltpu.VMEM((512, B), BF16),
             pltpu.VMEM((B, SLAB), BF16),
             pltpu.VMEM((B, SLAB), BF16),
             pltpu.VMEM((SLAB, B), F32),

time: 73.8 us -> 73.1 us (level)
  no operation moved by 1% of the time
where the time goes in v5:
time: 73.1 us; the launch traced here: 73 us
  Pallas kernels  72.3 us (99%)
    pallas_call x1, Pallas kernels, on_device(): pl.pallas_call(kernel, out_shape=shapes, in_specs=[anywhere, anywhere, pl...  70.5 us
    pallas_call x1, Pallas kernels, on_device(): pl.pallas_call(hand_over, out_shape=shapes, in_specs=[vmem, vmem], out_sp...  1.85 us

profile of v5, /device:TPU:1, one launch (start us, length us, event | category | flops | bytes accessed | tf_op | source)
XLA Modules:
  0.0 73.0 jit_solution(3688256214943517894)
XLA Ops:
  0.6 70.5 %shard_map.59 = (f32[480,256]{1,0:T(8,128)}, f32[1,32,256]{2,1,0:T(8,128)}) custom-call(f32[60,480]{1,0:T(8,128)} %bitcast.1, f32[480,256]{1,0:T(8,128)} %f_ref.1, s32[1,11]{1,0:T(1,128)} %s_ref.1, f32[1,32,256]{2,1,0:T(8,128)} %d_ref.1), custom_call_target="tpu_custom_call" | custom-call | tf_op jit(solution)/shard_map/pallas_call | solution.py:546
  71.1 1.8 %shard_map.60 = (f32[480,256]{1,0:T(8,128)}, f32[1,32,256]{2,1,0:T(8,128)}) custom-call(f32[480,256]{1,0:T(8,128)} %get-tuple-element.4.sel_ref, f32[1,32,256]{2,1,0:T(8,128)} %get-tuple-element.5.diag_ref), custom_call_target="tpu_custom_call" | custom-call | tf_op jit(solution)/shard_map/pallas_call | solution.py:595

commit v6 on v5

--- a/solution.py
+++ b/solution.py
@@ -401,7 +401,7 @@
         acc[...] += dot3((ah[j, :, lanes], al[j, :, lanes]), (fph[...], fpl[...]), ((1,), (0,)))
 
     def whole(t):
-        def body(s, carry):
+        for s in range(2):
             near = jnp.where(t == 0, 0, -2)
             odd = jnp.where(t == 0, -1, 1)
             j = 2 * div(zz(jnp.where(eq, near, odd)), 2) + s
@@ -412,12 +412,9 @@
                 if k % 2:
                     value = pltpu.roll(value, 60, 0)
                 high, rest = split(jnp.where(keep, value, 0.0))
-                fwh[64 * k : 64 * k + 64, :] = high
-                fwl[64 * k : 64 * k + 64, :] = rest
-            acc[...] += dot3((ah[j], al[j]), (fwh[...], fwl[...]), ((1,), (0,)))
-            return carry
-
-        lax.fori_loop(0, 2, body, 0)
+                fwh[s, 64 * k : 64 * k + 64, :] = high
+                fwl[s, 64 * k : 64 * k + 64, :] = rest
+            acc[...] += dot3((ah[j], al[j]), (fwh[s], fwl[s]), ((1,), (0,)))
 
     def products(count, pick):
         def body(i, carry):
@@ -563,8 +560,8 @@
             pltpu.VMEM((8, SLAB, B), F32),
             pltpu.VMEM((256, B), BF16),
             pltpu.VMEM((256, B), BF16),
-            pltpu.VMEM((512, B), BF16),
-            pltpu.VMEM((512, B), BF16),
+            pltpu.VMEM((2, 512, B), BF16),
+            pltpu.VMEM((2, 512, B), BF16),
             pltpu.VMEM((B, SLAB), BF16),
             pltpu.VMEM((B, SLAB), BF16),
             pltpu.VMEM((SLAB, B), F32),

time: 73.1 us -> 74.2 us (1.015)
  Pallas kernels: 72.3 us -> 73.3 us
    pallas_call x1, Pallas kernels: 70.5 us -> 71.5 us  [on_device(): pl.pallas_call(kernel, out_shape=shapes, in_specs=[anywhere, anywhere, pl...]
where the time goes in v6:
time: 74.2 us; the launch traced here: 74 us
  Pallas kernels  73.3 us (99%)
    pallas_call x1, Pallas kernels, on_device(): pl.pallas_call(kernel, out_shape=shapes, in_specs=[anywhere, anywhere, pl...  71.5 us
    pallas_call x1, Pallas kernels, on_device(): pl.pallas_call(hand_over, out_shape=shapes, in_specs=[vmem, vmem], out_sp...  1.85 us

profile of v6, /device:TPU:1, one launch (start us, length us, event | category | flops | bytes accessed | tf_op | source)
XLA Modules:
  0.0 74.0 jit_solution(1737884292817834329)
XLA Ops:
  0.6 71.5 %shard_map.59 = (f32[480,256]{1,0:T(8,128)}, f32[1,32,256]{2,1,0:T(8,128)}) custom-call(f32[60,480]{1,0:T(8,128)} %bitcast.1, f32[480,256]{1,0:T(8,128)} %f_ref.1, s32[1,11]{1,0:T(1,128)} %s_ref.1, f32[1,32,256]{2,1,0:T(8,128)} %d_ref.1), custom_call_target="tpu_custom_call" | custom-call | tf_op jit(solution)/shard_map/pallas_call | solution.py:543
  72.1 1.8 %shard_map.60 = (f32[480,256]{1,0:T(8,128)}, f32[1,32,256]{2,1,0:T(8,128)}) custom-call(f32[480,256]{1,0:T(8,128)} %get-tuple-element.4.sel_ref, f32[1,32,256]{2,1,0:T(8,128)} %get-tuple-element.5.diag_ref), custom_call_target="tpu_custom_call" | custom-call | tf_op jit(solution)/shard_map/pallas_call | solution.py:592
